TPU v7x, 32 devices: a whole 2x2x4 slice. The times are simulated.
32 devices in a mesh: groups: 2 (over y), blk: 16 (over z, x, core).
Axes of the slice: x: 2, y: 2, z: 4, core: 2. Of those that a mesh axis runs over, the one named last changes fastest.
Arguments:
- psi: bfloat16 [64, 512, 512], P(('groups', 'blk')), parts along dimension 0, may hold values from -6 to 6
- sector_size: int32 [64], P('groups'), parts along dimension 0, may hold values from 1 to 512, 8192 in all
- source: int32 [32, 32], P('groups'), parts along dimension 0, may hold values from 0 to 31, each once within a row
- left_env: bfloat16 [16, 64, 512], P(None, 'groups', 'blk'), parts along dimension 1, may hold values from -3 to 3
- right_env: bfloat16 [32, 512, 512], P('groups'), parts along dimension 0, may hold values from -0.25 to 0.25
Outputs:
- hpsi: bfloat16 [64, 512, 512], P(('groups', 'blk')), parts along dimension 0
There are 2 independent parts, one for each index of `groups`. A program takes and returns all parts, laid end to end along the dimension named above; each array names one. Nothing has to cross between parts.
Inputs may be any that keep to these rules, and one draw needn't show every extreme that they name: Each row of source is a permutation of the 32 sector blocks. `sector_size`: the sizes sum to 8192.
All inputs are finite; a program needn't handle non-finite values.
Results may differ from a plain program's by a relative error of at most 0.0049.
Values may be sent and summed in bfloat16 or wider, within the bound.
A program may use at most 128 MiB of HBM per device.

v0:
```python
import jax
import jax.numpy as jnp
from jax import lax
from jax.sharding import PartitionSpec as P


def local(psi, sector_size, source, left_env, right_env):
    nblk = lax.axis_size("blk")
    me_idx = lax.axis_index("blk")
    sec_local = psi.shape[0]
    rows_all = psi.shape[1]
    width = psi.shape[2]
    sectors = sector_size.shape[0]
    per_rows = rows_all // nblk
    own_sizes = lax.dynamic_slice_in_dim(sector_size, me_idx * sec_local, sec_local)
    rows = jnp.arange(rows_all, dtype=jnp.int32)
    keep = rows[None, :] < own_sizes[:, None]
    masked = jnp.where(keep[:, :, None], psi, jnp.zeros_like(psi))
    shaped = masked.reshape(sec_local, nblk, per_rows, width)
    moved = lax.all_to_all(shaped, "blk", split_axis=1, concat_axis=0, tiled=True)
    moved = moved.reshape(sectors, per_rows, width)
    gathered = moved[source]
    picked = jnp.einsum(
        "wsrk,wkj->wsrj", gathered, right_env, preferred_element_type=jnp.float32
    ).astype(jnp.bfloat16)
    coeff = left_env.astype(jnp.float32)
    total = jnp.einsum("wsr,wsrj->srj", coeff, picked.astype(jnp.float32))
    global_rows = me_idx * per_rows + jnp.arange(per_rows, dtype=jnp.int32)
    live = global_rows[None, :] < sector_size[:, None]
    result = jnp.where(live[:, :, None], total, jnp.zeros_like(total)).astype(jnp.bfloat16)
    result = result.reshape(sectors, 1, per_rows, width)
    back = lax.all_to_all(result, "blk", split_axis=0, concat_axis=1, tiled=True)
    return back.reshape(sec_local, rows_all, width)


def solution(mesh):
    return jax.shard_map(
        local,
        mesh=mesh,
        in_specs=(
            P(("groups", "blk"), None, None),
            P("groups"),
            P("groups", None),
            P(None, "groups", "blk"),
            P("groups", None, None),
        ),
        out_specs=P(("groups", "blk"), None, None),
        check_vma=False,
    )
```

profile of v0, /device:TPU:1, one launch (start us, length us, event | category | flops | bytes accessed | tf_op | source)
XLA Modules:
  0.0 115.5 jit_solution(7937954376797012406)
XLA Ops:
  0.0 0.7 dynamic_slice.3
  0.7 0.1 iota_compare_fusion
  0.8 1.4 %broadcast_select_fusion = bf16[2,512,512]{2,1,0:T(8,128)(2,1)S(1)} fusion(bf16[2,512,512]{2,1,0:T(8,128)(2,1)} %param.5, pred[2,512]{1,0:T(4,128)(4,1)S(1)} %iota_compare_fusion), kind=kLoop, calls=%fused_computation.8 | loop fusion | flops 524288 | bytes 2098176 | tf_op jit(solution)/shard_map/jit(_where)/select_n | solution.py:18
  2.2 1.0 copy.8
  3.3 7.3 %all-to-all-start = ((bf16[2,16,32,512]{3,2,0,1:T(8,128)(2,1)}), bf16[2,16,32,512]{3,2,0,1:T(8,128)(2,1)S(1)}, u32[]{:S(2)}, u32[]{:S(2)}) async-start(bf16[2,16,32,512]{3,2,0,1:T(8,128)(2,1)} %copy.8), calls=%async_computation | async-start | bytes 2097152 | tf_op jit(solution)/shard_map/all_to_all | solution.py:20
  10.6 0.7 compare_select_fusion
  11.3 0.1 reshape.73
  11.4 1.4 %copy.12 = bf16[16,32,32,1]{0,3,2,1:T(2,128)(2,1)S(1)} copy(bf16[16,32,32,1]{2,1,0,3:T(8,128)(2,1)} %bitcast.31) | data formatting | bytes 65536 | tf_op args[3]
  12.8 0.7 broadcast_compare_fusion
  13.6 20.2 %all-to-all-done = bf16[2,16,32,512]{3,2,0,1:T(8,128)(2,1)S(1)} async-done(((bf16[2,16,32,512]{3,2,0,1:T(8,128)(2,1)}), bf16[2,16,32,512]{3,2,0,1:T(8,128)(2,1)S(1)}, u32[]{:S(2)}, u32[]{:S(2)}) %all-to-all-start) | async-done | bytes 1048608 | tf_op jit(solution)/shard_map/all_to_all | solution.py:20
  33.7 13.9 %gather_fusion = bf16[512,32,512]{2,1,0:T(8,128)(2,1)} fusion(bf16[32,32,512]{2,1,0:T(8,128)(2,1)S(1)} %bitcast.27, s32[1024]{0:T(1024)S(1)} %pad_clamp_fusion), kind=kCustom, calls=%fused_computation | custom fusion | bytes 33556480 | tf_op jit(solution)/shard_map/gather | solution.py:22
  47.6 18.1 %convolution_convert_fusion = bf16[16,32,32,512]{3,2,1,0:T(8,128)(2,1)} fusion(bf16[16,32,32,512]{3,2,1,0:T(8,128)(2,1)} %bitcast.28, bf16[16,512,512]{2,1,0:T(8,128)(2,1)} %param.9), kind=kOutput, calls=%fused_computation.3 | convolution fusion | flops 8598323200 | bytes 41943040 | tf_op jit(solution)/shard_map/wsrk,wkj->wsrj/dot_general | solution.py:23
  65.8 16.6 %fusion = bf16[32,32,1,512]{3,2,1,0:T(2,128)(2,1)S(1)} fusion(bf16[16,32,32,1]{0,3,2,1:T(2,128)(2,1)S(1)} %copy.12, bf16[16,32,32,512]{3,2,1,0:T(8,128)(2,1)} %convolution_convert_fusion), kind=kOutput, calls=%fused_computation.1 | convolution fusion | flops 16777216 | bytes 17858560 | tf_op jit(solution)/shard_map/wsr,wsrj->srj/dot_general | solution.py:27
  82.4 0.4 fusion.4
  82.8 31.7 %all_to_all.30 = bf16[32,1,32,512]{3,2,1,0:T(8,128)(2,1)S(1)} all-to-all(bf16[32,1,32,512]{3,2,1,0:T(8,128)(2,1)S(1)} %fusion.4), channel_id=1, replica_groups=mesh['groups'=2,'blk'=16] {'blk'}, dimensions={0} | all-to-all | bytes 2097152 | tf_op jit(solution)/shard_map/all_to_all | solution.py:32
  114.5 1.0 copy.9
  (2 shorter events, 0.0 us)
Async XLA Ops:
  3.3 30.5 %all-to-all-start = ((bf16[2,16,32,512]{3,2,0,1:T(8,128)(2,1)}), bf16[2,16,32,512]{3,2,0,1:T(8,128)(2,1)S(1)}, u32[]{:S(2)}, u32[]{:S(2)}) async-start(bf16[2,16,32,512]{3,2,0,1:T(8,128)(2,1)} %copy.8), calls=%async_computation | async-start | bytes 2097152 | tf_op jit(solution)/shard_map/all_to_all | solution.py:20
where the time goes:
time: 116 us
  matrix products  34.7 us (30%)
  blocking collectives  31.7 us (27%)
  waiting for transfers between devices  20.2 us (17%)
  local copies, waits for them, and re-layouts  18.2 us (16%)
  starting transfers between devices  7.32 us (6%)
  other arithmetic  3.39 us (3%)
    all_to_all x1, blocking collectives, local(): lax.all_to_all(result, 'blk', split_axis=0, concat_axis=1, tiled=True)  31.7 us
    all_to_all x1, waiting for transfers between devices, local(): lax.all_to_all(shaped, 'blk', split_axis=1, concat_axis=0, tiled=True)  20.2 us
    dot_general x1, matrix products, local(): jnp.einsum('wsrk,wkj->wsrj', gathered, right_env, preferred_element_type=...  18.1 us
    dot_general x1, matrix products, local(): total = jnp.einsum('wsr,wsrj->srj', coeff, picked.astype(jnp.float32))  16.6 us
    gather x1, local copies, waits for them, and re-layouts, local(): gathered = moved[source]  13.9 us
    all_to_all x1, starting transfers between devices, local(): lax.all_to_all(shaped, 'blk', split_axis=1, concat_axis=0, tiled=True)  7.32 us
  transfers between devices with their start and end apart: 1, of which 1 were waited for; matrix products, arithmetic and copies ran while one was open for 3% of the time, Pallas kernels for 0%

commit v1 on v0

--- a/solution.py
+++ b/solution.py
@@ -1,15 +1,179 @@
+import functools
+
 import jax
 import jax.numpy as jnp
 from jax import lax
+from jax.experimental import pallas as pl
+from jax.experimental.pallas import tpu as pltpu
 from jax.sharding import PartitionSpec as P
 
-
-def local(psi, sector_size, source, left_env, right_env):
+MESH = pl.DeviceIdType.MESH
+CHUNK = 16
+LANES = 128
+
+
+def kernel(n, sizes, source, left, psi, right, out, recv, moved, res, coef, lhs, weights, fs, fr, bs, br, ls, lb, ws):
+    me = lax.axis_index("blk")
+    own, rows_all, width = psi.shape
+    terms, sectors = source.shape
+    per_rows = rows_all // n
+    chunks = per_rows // CHUNK
+
+    def peer_of(step):
+        shift = n // 2 + (1 - 2 * (step % 2)) * ((step + 1) // 2)
+        return lax.rem(me + shift, n)
+
+    def slot(device):
+        return pl.ds(device * own, own)
+
+    def rows_of(device, c):
+        return pl.ds(pl.multiple_of(device * per_rows + c * CHUNK, CHUNK), CHUNK)
+
+    def forward(c, peer, landing):
+        return pltpu.make_async_remote_copy(
+            src_ref=psi.at[:, rows_of(peer, c), :],
+            dst_ref=recv.at[c, slot(landing)],
+            send_sem=fs.at[c, peer],
+            recv_sem=fr.at[c, landing],
+            device_id={"blk": peer},
+            device_id_type=MESH,
+        )
+
+    def backward(c, peer, landing):
+        return pltpu.make_async_remote_copy(
+            src_ref=res.at[c, slot(peer)],
+            dst_ref=out.at[:, rows_of(landing, c), :],
+            send_sem=bs.at[c, peer],
+            recv_sem=br.at[c, landing],
+            device_id={"blk": peer},
+            device_id_type=MESH,
+        )
+
+    def own_in(c):
+        return pltpu.make_async_copy(psi.at[:, rows_of(me, c), :], recv.at[c, slot(me)], ls.at[c])
+
+    def own_out(c):
+        return pltpu.make_async_copy(res.at[c, slot(me)], out.at[:, rows_of(me, c), :], lb.at[c])
+
+    def each_peer(action):
+        def step(k, carry):
+            action(peer_of(k))
+            return carry
+
+        lax.fori_loop(0, n - 1, step, 0)
+
+    load = pltpu.make_async_copy(right, weights, ws)
+    barrier = pltpu.get_barrier_semaphore()
+    each_peer(lambda peer: pl.semaphore_signal(barrier, inc=1, device_id={"blk": peer}, device_id_type=MESH))
+    pl.semaphore_wait(barrier, n - 1)
+
+    for c in range(chunks):
+        each_peer(lambda peer: forward(c, peer, me).start())
+    for c in range(chunks):
+        own_in(c).start()
+    load.start()
+
+    row = lax.broadcasted_iota(jnp.int32, (per_rows, LANES), 0) + me * per_rows
+    unit = (
+        lax.broadcasted_iota(jnp.int32, (per_rows, per_rows), 0)
+        == lax.broadcasted_iota(jnp.int32, (per_rows, per_rows), 1)
+    ).astype(jnp.float32).astype(jnp.bfloat16)
+
+    def spread(w, carry):
+        turned = lax.dot_general(
+            unit, left[w], (((1,), (1,)), ((), ())), preferred_element_type=jnp.float32
+        )
+        for s in range(sectors):
+            column = jnp.broadcast_to(turned[:, s : s + 1], (per_rows, LANES))
+            coef[w, s] = jnp.where(row < sizes[s], column, 0.0).astype(jnp.bfloat16)
+        return carry
+
+    lax.fori_loop(0, terms, spread, 0)
+
+    row16 = lax.broadcasted_iota(jnp.int32, (CHUNK, width), 0) + me * per_rows
+    for c in range(chunks):
+        own_in(c).wait()
+        each_peer(lambda peer: forward(c, peer, peer).wait_recv())
+
+        def mask(s, carry):
+            value = recv[c, s].astype(jnp.float32)
+            moved[s] = jnp.where(row16 + c * CHUNK < sizes[s], value, 0.0).astype(jnp.bfloat16)
+            return carry
+
+        lax.fori_loop(0, sectors, mask, 0)
+
+        def build(w, carry):
+            columns = pl.ds(pl.multiple_of(w * width, width), width)
+            for s in range(sectors):
+                factor = coef[w, s, c * CHUNK : (c + 1) * CHUNK, :]
+                factor = jnp.concatenate([factor] * (width // LANES), axis=1)
+                lhs[s * CHUNK : (s + 1) * CHUNK, columns] = moved[source[w, s]] * factor
+            return carry
+
+        lax.fori_loop(0, terms, build, 0)
+        if c == 0:
+            load.wait()
+        tall = weights.reshape(terms * width, width)
+        half = width // 2
+        for part in range(2):
+            cols = slice(part * half, (part + 1) * half)
+            total = jnp.dot(lhs[...], tall[:, cols], preferred_element_type=jnp.float32)
+            res[c, :, :, cols] = total.astype(jnp.bfloat16).reshape(sectors, CHUNK, half)
+        each_peer(lambda peer: backward(c, peer, me).start())
+        own_out(c).start()
+
+    for c in range(chunks):
+        each_peer(lambda peer: forward(c, peer, me).wait_send())
+        each_peer(lambda peer: backward(c, peer, me).wait_send())
+        own_out(c).wait()
+        each_peer(lambda peer: backward(c, peer, peer).wait_recv())
+
+
+def fused(psi, sector_size, source, left_env, right_env):
+    n = lax.axis_size("blk")
+    own, rows_all, width = psi.shape
+    terms, sectors = source.shape
+    per_rows = rows_all // n
+    chunks = per_rows // CHUNK
+    rows = sectors * CHUNK
+    smem = pl.BlockSpec(memory_space=pltpu.SMEM)
+    vmem = pl.BlockSpec(memory_space=pltpu.VMEM)
+    anywhere = pl.BlockSpec(memory_space=pl.ANY)
+    return pl.pallas_call(
+        functools.partial(kernel, n),
+        out_shape=jax.ShapeDtypeStruct(psi.shape, jnp.bfloat16),
+        in_specs=[smem, smem, vmem, anywhere, anywhere],
+        out_specs=anywhere,
+        scratch_shapes=[
+            pltpu.VMEM((chunks, sectors, CHUNK, width), jnp.bfloat16),
+            pltpu.VMEM((sectors, CHUNK, width), jnp.bfloat16),
+            pltpu.VMEM((chunks, sectors, CHUNK, width), jnp.bfloat16),
+            pltpu.VMEM((terms, sectors, per_rows, LANES), jnp.bfloat16),
+            pltpu.VMEM((rows, terms * width), jnp.bfloat16),
+            pltpu.VMEM((terms, width, width), jnp.bfloat16),
+            pltpu.SemaphoreType.DMA((chunks, n)),
+            pltpu.SemaphoreType.DMA((chunks, n)),
+            pltpu.SemaphoreType.DMA((chunks, n)),
+            pltpu.SemaphoreType.DMA((chunks, n)),
+            pltpu.SemaphoreType.DMA((chunks,)),
+            pltpu.SemaphoreType.DMA((chunks,)),
+            pltpu.SemaphoreType.DMA,
+        ],
+        compiler_params=pltpu.CompilerParams(
+            collective_id=0, has_side_effects=True, vmem_limit_bytes=48 << 20
+        ),
+        cost_estimate=pl.CostEstimate(
+            flops=2 * terms * sectors * per_rows * width * width,
+            bytes_accessed=right_env.size * 2 + psi.size * 8,
+            transcendentals=0,
+        ),
+    )(sector_size, source, left_env, psi, right_env)
+
+
+def plain(psi, sector_size, source, left_env, right_env):
     nblk = lax.axis_size("blk")
     me_idx = lax.axis_index("blk")
-    sec_local = psi.shape[0]
-    rows_all = psi.shape[1]
-    width = psi.shape[2]
+    sec_local, rows_all, width = psi.shape
     sectors = sector_size.shape[0]
     per_rows = rows_all // nblk
     own_sizes = lax.dynamic_slice_in_dim(sector_size, me_idx * sec_local, sec_local)
@@ -33,6 +197,12 @@
     return back.reshape(sec_local, rows_all, width)
 
 
+def local(psi, sector_size, source, left_env, right_env):
+    per_rows = psi.shape[1] // lax.axis_size("blk")
+    run = fused if per_rows % CHUNK == 0 else plain
+    return run(psi, sector_size, source, left_env, right_env)
+
+
 def solution(mesh):
     return jax.shard_map(
         local,

time: 116 us -> 59.7 us (0.51)
  Pallas kernels: 0 us -> 54 us
  matrix products: 34.7 us -> 0 us
  blocking collectives: 31.7 us -> 0 us
  waiting for transfers between devices: 20.2 us -> 0 us
  local copies, waits for them, and re-layouts: 18.2 us -> 4.45 us
  starting transfers between devices: 7.32 us -> 0 us
  other arithmetic: 3.39 us -> 0 us
    pallas_call x0 -> x1, Pallas kernels: none -> 54 us  [fused(): pl.pallas_call(functools.partial(kernel, n), out_shape=jax.ShapeDtypeStru...]
    dot_general x2 -> x0, matrix products: 34.7 us -> none  [the longest x1 18.1 us: local(): jnp.einsum('wsrk,wkj->wsrj', gathered, right_env, preferred_element_type=...]
    all_to_all x1 -> x0, blocking collectives: 31.7 us -> none  [local(): lax.all_to_all(result, 'blk', split_axis=0, concat_axis=1, tiled=True)]
    all_to_all x1 -> x0, waiting for transfers between devices: 20.2 us -> none  [local(): lax.all_to_all(shaped, 'blk', split_axis=1, concat_axis=0, tiled=True)]
    gather x1 -> x0, local copies, waits for them, and re-layouts: 13.9 us -> none  [local(): gathered = moved[source]]
    all_to_all x1 -> x0, starting transfers between devices: 7.32 us -> none  [local(): lax.all_to_all(shaped, 'blk', split_axis=1, concat_axis=0, tiled=True)]
    unnamed x1 -> x9, local copies, waits for them, and re-layouts: 1.43 us -> 4.45 us
    select_n x2 -> x0, other arithmetic: 2.12 us -> none  [the longest x1 1.43 us: local(): masked = jnp.where(keep[:, :, None], psi, jnp.zeros_like(psi))]
  transfers between devices with their start and end apart: 1 -> 0, of which waited for: 1 -> 0; matrix products, arithmetic and copies ran while one was open for 3% -> 0% of each run, Pallas kernels for 0% -> 0%
where the time goes in v1:
time: 59.7 us; the launch traced here: 58.5 us
  Pallas kernels  54 us (90%)
  local copies, waits for them, and re-layouts  4.45 us (7%)
    pallas_call x1, Pallas kernels, fused(): pl.pallas_call(functools.partial(kernel, n), out_shape=jax.ShapeDtypeStru...  54 us
    unnamed x9, local copies, waits for them, and re-layouts  4.45 us

profile of v1, /device:TPU:1, one launch (start us, length us, event | category | flops | bytes accessed | tf_op | source)
XLA Modules:
  0.0 58.5 jit_solution(495074746358563215)
XLA Ops:
  0.0 0.0 copy-start
  0.0 1.2 %copy-done = bf16[2,512,512]{2,1,0:T(8,128)(2,1)S(1)} copy-done((bf16[2,512,512]{2,1,0:T(8,128)(2,1)S(1)}, bf16[2,512,512]{2,1,0:T(8,128)(2,1)}, u32[]{:S(2)}) %copy-start) | copy-done | bytes 1048600
  1.2 0.0 copy-start.1
  1.2 0.9 %copy-done.1 = bf16[16,32,32]{2,1,0:T(8,128)(2,1)S(1)} copy-done((bf16[16,32,32]{2,1,0:T(8,128)(2,1)S(1)}, bf16[16,32,32]{2,1,0:T(8,128)(2,1)}, u32[]{:S(2)}) %copy-start.1) | copy-done | bytes 32792
  2.1 0.0 copy-start.2
  2.1 0.7 %copy-done.2 = s32[16,32]{1,0:T(8,128)S(1)} copy-done((s32[16,32]{1,0:T(8,128)S(1)}, s32[16,32]{1,0:T(8,128)}, u32[]{:S(2)}) %copy-start.2) | copy-done | bytes 2072
  2.8 0.0 copy-start.3
  2.8 0.7 %copy-done.3 = s32[32]{0:T(128)S(1)} copy-done((s32[32]{0:T(128)S(1)}, s32[32]{0:T(128)}, u32[]{:S(2)}) %copy-start.3) | copy-done | bytes 152
  3.5 54.0 %shard_map.55 = bf16[2,512,512]{2,1,0:T(8,128)(2,1)S(1)} custom-call(s32[32]{0:T(128)S(1)} %copy-done.3, s32[16,32]{1,0:T(8,128)S(1)} %copy-done.2, bf16[16,32,32]{2,1,0:T(8,128)(2,1)S(1)} %copy-done.1, bf16[2,512,512]{2,1,0:T(8,128)(2,1)S(1)} %copy-done, bf16[16,512,512]{2,1,0:T(8,128)(2,1)} %right.1), custom_call_target="tpu_custom_call" | custom-call | flops 8589934592 | bytes 12582912 | tf_op jit(solution)/shard_map/pallas_call | solution.py:142
  57.5 1.0 %copy.7 = bf16[2,512,512]{2,1,0:T(8,128)(2,1)} copy(bf16[2,512,512]{2,1,0:T(8,128)(2,1)S(1)} %shard_map.55) | data formatting | bytes 2097152
Async XLA Ops:
  0.0 1.2 %copy-start = (bf16[2,512,512]{2,1,0:T(8,128)(2,1)S(1)}, bf16[2,512,512]{2,1,0:T(8,128)(2,1)}, u32[]{:S(2)}) copy-start(bf16[2,512,512]{2,1,0:T(8,128)(2,1)} %psi.1) | copy-start | bytes 3145732
  1.2 0.9 %copy-start.1 = (bf16[16,32,32]{2,1,0:T(8,128)(2,1)S(1)}, bf16[16,32,32]{2,1,0:T(8,128)(2,1)}, u32[]{:S(2)}) copy-start(bf16[16,32,32]{2,1,0:T(8,128)(2,1)} %left.1) | copy-start | bytes 98308
  2.1 0.7 %copy-start.2 = (s32[16,32]{1,0:T(8,128)S(1)}, s32[16,32]{1,0:T(8,128)}, u32[]{:S(2)}) copy-start(s32[16,32]{1,0:T(8,128)} %source.1) | copy-start | bytes 6148
  2.8 0.7 %copy-start.3 = (s32[32]{0:T(128)S(1)}, s32[32]{0:T(128)}, u32[]{:S(2)}) copy-start(s32[32]{0:T(128)} %sizes.1) | copy-start | bytes 388

commit v2 on v1

--- a/solution.py
+++ b/solution.py
@@ -12,7 +12,10 @@
 LANES = 128
 
 
-def kernel(n, sizes, source, left, psi, right, out, recv, moved, res, coef, lhs, weights, fs, fr, bs, br, ls, lb, ws):
+def kernel(
+    n, sizes_in, source_in, left_in, psi, right, out,
+    sizes, source, left, recv, moved, res, coef, lhs, weights, fs, fr, bs, br, ls, lb, ws, os,
+):
     me = lax.axis_index("blk")
     own, rows_all, width = psi.shape
     terms, sectors = source.shape
@@ -20,8 +23,7 @@
     chunks = per_rows // CHUNK
 
     def peer_of(step):
-        shift = n // 2 + (1 - 2 * (step % 2)) * ((step + 1) // 2)
-        return lax.rem(me + shift, n)
+        return lax.rem(me + 1 + step, n)
 
     def slot(device):
         return pl.ds(device * own, own)
@@ -63,15 +65,24 @@
         lax.fori_loop(0, n - 1, step, 0)
 
     load = pltpu.make_async_copy(right, weights, ws)
+    operands = [
+        pltpu.make_async_copy(sizes_in, sizes, os.at[0]),
+        pltpu.make_async_copy(source_in, source, os.at[1]),
+        pltpu.make_async_copy(left_in, left, os.at[2]),
+    ]
     barrier = pltpu.get_barrier_semaphore()
     each_peer(lambda peer: pl.semaphore_signal(barrier, inc=1, device_id={"blk": peer}, device_id_type=MESH))
+    for c in range(chunks):
+        own_in(c).start()
+    for operand in operands:
+        operand.start()
     pl.semaphore_wait(barrier, n - 1)
 
     for c in range(chunks):
         each_peer(lambda peer: forward(c, peer, me).start())
-    for c in range(chunks):
-        own_in(c).start()
     load.start()
+    for operand in operands:
+        operand.wait()
 
     row = lax.broadcasted_iota(jnp.int32, (per_rows, LANES), 0) + me * per_rows
     unit = (
@@ -136,15 +147,16 @@
     per_rows = rows_all // n
     chunks = per_rows // CHUNK
     rows = sectors * CHUNK
-    smem = pl.BlockSpec(memory_space=pltpu.SMEM)
-    vmem = pl.BlockSpec(memory_space=pltpu.VMEM)
     anywhere = pl.BlockSpec(memory_space=pl.ANY)
     return pl.pallas_call(
         functools.partial(kernel, n),
         out_shape=jax.ShapeDtypeStruct(psi.shape, jnp.bfloat16),
-        in_specs=[smem, smem, vmem, anywhere, anywhere],
+        in_specs=[anywhere] * 5,
         out_specs=anywhere,
         scratch_shapes=[
+            pltpu.SMEM(sector_size.shape, jnp.int32),
+            pltpu.SMEM(source.shape, jnp.int32),
+            pltpu.VMEM(left_env.shape, jnp.bfloat16),
             pltpu.VMEM((chunks, sectors, CHUNK, width), jnp.bfloat16),
             pltpu.VMEM((sectors, CHUNK, width), jnp.bfloat16),
             pltpu.VMEM((chunks, sectors, CHUNK, width), jnp.bfloat16),
@@ -158,9 +170,10 @@
             pltpu.SemaphoreType.DMA((chunks,)),
             pltpu.SemaphoreType.DMA((chunks,)),
             pltpu.SemaphoreType.DMA,
+            pltpu.SemaphoreType.DMA((3,)),
         ],
         compiler_params=pltpu.CompilerParams(
-            collective_id=0, has_side_effects=True, vmem_limit_bytes=48 << 20
+            collective_id=0, has_side_effects=True, vmem_limit_bytes=62 << 20
         ),
         cost_estimate=pl.CostEstimate(
             flops=2 * terms * sectors * per_rows * width * width,

time: 59.7 us -> 55.3 us (0.926)
  the two profiles are of different devices: /device:TPU:1 before, /device:TPU:31 now
where the time goes in v2:
time: 55.3 us; the launch traced here: 55.2 us
  Pallas kernels  52.9 us (96%)
  local copies, waits for them, and re-layouts  2.26 us (4%)
    pallas_call x1, Pallas kernels, fused(): pl.pallas_call(functools.partial(kernel, n), out_shape=jax.ShapeDtypeStru...  52.9 us
    unnamed x1, local copies, waits for them, and re-layouts  2.26 us

profile of v2, /device:TPU:31, one launch (start us, length us, event | category | flops | bytes accessed | tf_op | source)
XLA Modules:
  0.0 55.2 jit_solution(1252911262840916748)
XLA Ops:
  0.0 52.9 %shard_map.55 = bf16[2,512,512]{2,1,0:T(8,128)(2,1)} custom-call(s32[32]{0:T(128)} %sizes_in.1, s32[16,32]{1,0:T(8,128)} %source_in.1, bf16[16,32,32]{2,1,0:T(8,128)(2,1)} %left_in.1, bf16[2,512,512]{2,1,0:T(8,128)(2,1)} %psi.1, bf16[16,512,512]{2,1,0:T(8,128)(2,1)} %right.1), custom_call_target="tpu_custom_call" | custom-call | flops 8589934592 | bytes 12582912 | tf_op jit(solution)/shard_map/pallas_call | solution.py:151
  52.9 2.3 %copy.7 = bf16[2,512,512]{2,1,0:T(8,128)(2,1)} copy(bf16[2,512,512]{2,1,0:T(8,128)(2,1)} %shard_map.55) | data formatting | bytes 2097152

commit v3 on v2

--- a/solution.py
+++ b/solution.py
@@ -23,7 +23,13 @@
     chunks = per_rows // CHUNK
 
     def peer_of(step):
-        return lax.rem(me + 1 + step, n)
+        if n % 4:
+            return lax.rem(me + 1 + step, n)
+        k = step + 1
+        z = lax.rem(me // 4 + k // 4, n // 4)
+        x = lax.rem((me % 4) // 2 + (k % 4) // 2, 2)
+        core = lax.rem(me % 2 + k % 2, 2)
+        return z * 4 + x * 2 + core
 
     def slot(device):
         return pl.ds(device * own, own)

time: 55.3 us -> 54.8 us (level)
  the two profiles are of different devices: /device:TPU:31 before, /device:TPU:17 now
where the time goes in v3:
time: 54.8 us; the launch traced here: 54.6 us
  Pallas kernels  52.4 us (96%)
  local copies, waits for them, and re-layouts  2.26 us (4%)
    pallas_call x1, Pallas kernels, fused(): pl.pallas_call(functools.partial(kernel, n), out_shape=jax.ShapeDtypeStru...  52.4 us
    unnamed x1, local copies, waits for them, and re-layouts  2.26 us

profile of v3, /device:TPU:17, one launch (start us, length us, event | category | flops | bytes accessed | tf_op | source)
XLA Modules:
  0.0 54.6 jit_solution(3344635891708386334)
XLA Ops:
  0.0 52.4 %shard_map.55 = bf16[2,512,512]{2,1,0:T(8,128)(2,1)} custom-call(s32[32]{0:T(128)} %sizes_in.1, s32[16,32]{1,0:T(8,128)} %source_in.1, bf16[16,32,32]{2,1,0:T(8,128)(2,1)} %left_in.1, bf16[2,512,512]{2,1,0:T(8,128)(2,1)} %psi.1, bf16[16,512,512]{2,1,0:T(8,128)(2,1)} %right.1), custom_call_target="tpu_custom_call" | custom-call | flops 8589934592 | bytes 12582912 | tf_op jit(solution)/shard_map/pallas_call | solution.py:157
  52.4 2.3 %copy.7 = bf16[2,512,512]{2,1,0:T(8,128)(2,1)} copy(bf16[2,512,512]{2,1,0:T(8,128)(2,1)} %shard_map.55) | data formatting | bytes 2097152
